TPU v7x, 32 devices: a whole 2x2x4 slice. The times are simulated.
32 devices in a mesh: section: 2 (over core), fsdp: 16 (over z, y, x).
Axes of the slice: x: 2, y: 2, z: 4, core: 2. Of those that a mesh axis runs over, the one named last changes fastest.
Arguments:
- images: bfloat16 [2, 96, 197, 384], P(None, 'fsdp'), may hold values from -6 to 6
- cotangent: bfloat16 [2, 96, 197, 384], P(None, 'fsdp'), may hold values from -6 to 6
- counts: int32 [2, 16], P(None, 'fsdp'), may hold values from 1 to 6, 72 in all within a row
- ln1_gain: bfloat16 [2, 384], P('section', 'fsdp'), may hold values from 0.099609375 to 1.8984375
- ln1_bias: bfloat16 [2, 384], P('section', 'fsdp'), may hold values from -1.75 to 1.75
- w_qkv: bfloat16 [2, 384, 1152], P('section', 'fsdp'), may hold values from -0.4375 to 0.4375
- b_qv: bfloat16 [2, 768], P('section', 'fsdp'), may hold values from -3 to 3
- w_out: bfloat16 [2, 384, 384], P('section', 'fsdp'), may hold values from -0.875 to 0.875
- b_out: bfloat16 [2, 384], P('section', 'fsdp'), may hold values from -3 to 3
- ln2_gain: bfloat16 [2, 384], P('section', 'fsdp'), may hold values from 0.099609375 to 1.8984375
- ln2_bias: bfloat16 [2, 384], P('section', 'fsdp'), may hold values from -1.75 to 1.75
- w_up: bfloat16 [2, 384, 1536], P('section', 'fsdp'), may hold values from -0.3125 to 0.3125
- b_up: bfloat16 [2, 1536], P('section', 'fsdp'), may hold values from -3 to 3
- w_down: bfloat16 [2, 1536, 384], P('section', 'fsdp'), may hold values from -0.15625 to 0.15625
- b_down: bfloat16 [2, 384], P('section', 'fsdp'), may hold values from -3 to 3
Outputs:
- acts: bfloat16 [2, 2, 96, 197, 384], P('section', None, 'fsdp')
- in_grads: bfloat16 [2, 2, 96, 197, 384], P('section', None, 'fsdp')
- grad_ln1_gain: float32 [2, 384], P('section', 'fsdp')
- grad_ln1_bias: float32 [2, 384], P('section', 'fsdp')
- grad_w_qkv: float32 [2, 384, 1152], P('section', 'fsdp')
- grad_b_qv: float32 [2, 768], P('section', 'fsdp')
- grad_w_out: float32 [2, 384, 384], P('section', 'fsdp')
- grad_b_out: float32 [2, 384], P('section', 'fsdp')
- grad_ln2_gain: float32 [2, 384], P('section', 'fsdp')
- grad_ln2_bias: float32 [2, 384], P('section', 'fsdp')
- grad_w_up: float32 [2, 384, 1536], P('section', 'fsdp')
- grad_b_up: float32 [2, 1536], P('section', 'fsdp')
- grad_w_down: float32 [2, 1536, 384], P('section', 'fsdp')
- grad_b_down: float32 [2, 384], P('section', 'fsdp')
Inputs may be any that keep to these rules, and one draw needn't show every extreme that they name: counts[m, d] of the 6 image slots of fsdp index d in micro-batch m hold images, the first ones; each micro-batch holds 72 images, and in each some index holds 6.
All inputs are finite; a program needn't handle non-finite values. No bound on the sum of `counts` on one device may be relied on, other than what follows from the above.
Results may differ from a plain program's by a relative error of at most 0.02.
The roundings to bfloat16 on the way count: a program that leaves them out, or rounds other values in their place, can miss the bound.
Values may be sent and summed in bfloat16 or wider, within the bound.
A program may use at most 256 MiB of HBM per device.

v0:
```python
import functools
import math

import jax
import jax.numpy as jnp
from jax import lax
from jax.experimental import pallas as pl
from jax.experimental.pallas import tpu as pltpu
from jax.sharding import PartitionSpec as P

HEADS = 6
EPS = 1e-06
F32 = jnp.float32
LOW = jnp.bfloat16

G1, S1, BO, G2, S2, BD, BQ, BV, BU = 0, 1, 2, 3, 4, 5, 6, 7, 8
TABLE = 16
TOGETHER, TOGETHER_ROWS = 2, 2
ATT, UP, DOWN, TAB = 0, 1, 2, 3


def radices(n):
    rest = max(r for r in range(1, n + 1) if r * r * r <= n and n % (r * r) == 0)
    return n // (rest * rest), rest


def mm(left, right):
    return jnp.dot(left, right, preferred_element_type=F32)


def mm_right(left, right):
    return lax.dot_general(left, right, (((1,), (1,)), ((), ())), preferred_element_type=F32)


def mm_left(left, right):
    return lax.dot_general(left, right, (((0,), (0,)), ((), ())), preferred_element_type=F32)


def normal_parts(pre):
    phi = 0.5 + 0.5 * lax.erf(pre * 0.7071067811865476)
    low = pre.astype(LOW)
    density = jnp.exp2(low * low * LOW(-0.5 * 1.4426950408889634)) * LOW(0.3989422804014327)
    return phi, phi.astype(LOW) + low * density


def normalize(value):
    mean = jnp.mean(value, axis=-1, keepdims=True)
    center = value - mean
    rstd = lax.rsqrt(jnp.mean(center * center, axis=-1, keepdims=True) + EPS)
    return center * rstd, rstd, mean


def normalize_back(d_hat, hat, rstd):
    mean_one = jnp.mean(d_hat, axis=-1, keepdims=True)
    mean_two = jnp.mean(d_hat * hat, axis=-1, keepdims=True)
    return rstd * (d_hat - mean_one - hat * mean_two)


def colsum(value):
    return jnp.sum(value, axis=0, keepdims=True)


def whole_kernel(dims, *refs):
    slots, length, rows, width, ff, head_dim, n = dims
    (
        images, cotangent, counts, v_g1, v_s1, v_bo, v_g2, v_s2, v_bd, v_qv, v_up, a_qkv, a_out, a_up, a_down,
        woven, f_a, f_u, f_d, f_t, hid_far, slope_far, out_far,
        xs, raw, io_one, io_two, pack_a, pack_u, pack_d, pack_t,
        wqkv, wout, wup, wdown, table, gtable, rep_one, rep_two, rep_four,
        after_ref, nrm1, qkv, prob, overs, ctx, hat2, rstds, hid, slope, dal, low_g, left_t,
        s_a, s_u, s_d, s_t, r0_a, r0_u, r0_d, r0_t, r1_a, r1_u, r1_d, r1_t, r2_u, r2_d,
        r3_a, r3_u, r3_d, r3_t,
        in_s, weave_in, weave_out, ship_s, ship_r, far_s, ag1_s, ag1_r, ag2_s, ag2_r, ag3_s, ag3_r, ag4_s, ag4_r,
        rs0_s, rs0_r, rs1_s, rs1_r, rs2_s, rs2_r, rs3_s, rs3_r, credit,
    ) = refs
    groups = (ATT, UP, DOWN, TAB)
    pack = (pack_a, pack_u, pack_d, pack_t)
    stage = (s_a, s_u, s_d, s_t)
    r0, r1, r2 = (r0_a, r0_u, r0_d, r0_t), (r1_a, r1_u, r1_d, r1_t), (None, r2_u, r2_d, None)
    r3, final = (r3_a, r3_u, r3_d, r3_t), (f_a, f_u, f_d, f_t)

    first, rest = radices(n)
    unit = width // n
    core = lax.axis_index("section")
    me = lax.axis_index("fsdp")
    dig_a, dig_b, dig_c = me // (rest * rest), (me // rest) % rest, me % rest
    dig_three, dig_two = dig_c + core * (dig_b - dig_c), dig_b + core * (dig_c - dig_b)
    step_three, step_two = 1 + core * (rest - 1), rest - core * (rest - 1)
    pos = (dig_three * rest + dig_two) * first + dig_a
    pos_of = ((dig_c * rest + dig_b) * first + dig_a, (dig_b * rest + dig_c) * first + dig_a)
    sibling = {"section": 1 - core}

    def place(half, j):
        a, b, c = j // (rest * rest), (j // rest) % rest, j % rest
        return ((c * rest + b) if half == 0 else (b * rest + c)) * first + a

    def peer_first(t):
        return {"fsdp": me + ((dig_a + t) % first - dig_a) * (rest * rest)}

    def peer_two(t):
        return {"fsdp": me + ((dig_two + t) % rest - dig_two) * step_two}

    def peer_three(t):
        return {"fsdp": me + ((dig_three + t) % rest - dig_three) * step_three}

    def peer_plane(three, two):
        here = ((dig_three + three) % rest - dig_three) * step_three
        return {"fsdp": me + here + ((dig_two + two) % rest - dig_two) * step_two}

    plane = [(three, two) for three in range(rest) for two in range(rest) if three or two]

    def remote(src, dst, s_sem, r_sem, device):
        return pltpu.make_async_remote_copy(
            src_ref=src, dst_ref=dst, send_sem=s_sem, recv_sem=r_sem, device_id=device,
            device_id_type=pl.DeviceIdType.MESH,
        )

    def slab_two(three, two):
        return pl.ds((three * rest + two) * first, first)

    def slab_three(three):
        return pl.ds(three * rest * first, rest * first)

    def fill_repeats():
        for ref in (rep_one, rep_two, rep_four):
            part = ref.shape[0]
            lanes = lax.broadcasted_iota(jnp.int32, ref.shape, 1).astype(F32)
            line = lax.broadcasted_iota(jnp.int32, ref.shape, 0).astype(F32)
            rest_of = lanes - part * jnp.floor((lanes + 0.5) * (1.0 / part))
            ref[...] = jnp.where(jnp.abs(rest_of - line) < 0.5, 1.0, 0.0).astype(LOW)

    def own_lanes(part):
        shape = (n, part * n)
        lanes = lax.broadcasted_iota(jnp.int32, shape, 1)
        begin = lax.broadcasted_iota(jnp.int32, shape, 0) * part
        return (lanes >= begin) & (lanes < begin + part)

    shares = (
        ((G1, unit, rep_one), (S1, unit, rep_one), (BO, unit, rep_one), (G2, unit, rep_one), (S2, unit, rep_one),
         (BD, unit, rep_one), (BQ, 2 * unit, rep_two)),
        ((BU, 4 * unit, rep_four),),
    )

    def table_in(b):
        for half in range(2):
            lines = jnp.concatenate([s_t[b, half, place(half, j)] for j in range(n)], axis=0)
            begin = 0
            for row, part, ref in shares[half]:
                spread = mm(lines[:, begin : begin + part].astype(LOW), ref[...])
                line = colsum(jnp.where(own_lanes(part), spread, 0.0))
                for i in range(part * n // width):
                    table[b, row + i : row + i + 1, :] = line[:, width * i : width * (i + 1)]
                begin += part

    def table_out(b):
        for half in range(2):
            parts, begin = [], 0
            for row, part, ref in shares[half]:
                count = part * n // width
                line = jnp.concatenate([gtable[b, row + i : row + i + 1, :] for i in range(count)], axis=1)
                parts.append(mm_right(jnp.where(own_lanes(part), line, 0.0).astype(LOW), ref[...]))
                begin += part
            parts.append(jnp.zeros((n, width - begin), F32))
            lines = jnp.concatenate(parts, axis=1)
            for j in range(n):
                s_t[b, half, place(half, j)] = lines[j : j + 1]

    def pack_own():
        for half in range(2):
            vectors = ((v_g1, v_s1, v_bo, v_g2, v_s2, v_bd, v_qv), (v_up,))[half]
            lines = [vector[...].astype(F32) for vector in vectors]
            lines.append(jnp.zeros((1, width - sum(line.shape[1] for line in lines)), F32))
            pack_t[half] = jnp.concatenate(lines, axis=1)
            for ref in (pack_a, pack_u):
                both = []
                for part in (2 * half, 2 * half + 1):
                    if ref is pack_u:
                        both.append(a_up[0, :, part * width : (part + 1) * width])
                    elif part == 3:
                        both.append(a_out[0])
                    else:
                        both.append(a_qkv[0, :, part * width : (part + 1) * width])
                ref[half] = jnp.concatenate([value.astype(F32) for value in both], axis=0).astype(LOW)
            pack_d[half] = a_down[0, 2 * unit * half : 2 * unit * (half + 1), :]

    def at(b, g):
        return len(groups) * b + g

    def ag1_copy(b, g, half, t):
        device = {"section": half, **peer_first(t)} if t else sibling
        return remote(
            pack[g].at[half], stage[g].at[b, half, pos_of[half]],
            ag1_s.at[g, half, t], ag1_r.at[at(b, g), t], device,
        )

    def ag1_landing(b, g, t):
        ref = stage[g].at[b, core, (dig_three * rest + dig_two) * first + (dig_a + first - t) % first]
        return remote(ref, ref, ag1_s.at[g, 0, t], ag1_r.at[at(b, g), t], sibling)

    def ag2_copy(b, g, t):
        ref = stage[g].at[b, core, slab_two(dig_three, dig_two)]
        return remote(ref, ref, ag2_s.at[at(b, g), t - 1], ag2_r.at[at(b, g), t - 1], peer_two(t))

    def ag3_copy(b, g, t):
        ref = stage[g].at[b, core, slab_three(dig_three)]
        return remote(ref, ref, ag3_s.at[at(b, g), t - 1], ag3_r.at[at(b, g), t - 1], peer_three(t))

    def ag4_copy(b, g, t):
        ref = stage[g].at[b, core, slab_three((dig_three + rest - t) % rest)]
        return remote(ref, ref, ag4_s.at[at(b, g), t], ag4_r.at[at(b, g), t], sibling)

    def ag4_landing(b, g, t):
        ref = stage[g].at[b, 1 - core, slab_three((dig_two + rest - t) % rest)]
        return remote(ref, ref, ag4_s.at[at(b, g), t], ag4_r.at[at(b, g), t], sibling)

    def ag1(b, g):
        @pl.when(core == b)
        def _():
            for t in range(1, first):
                for half in range(2):
                    ag1_copy(b, g, half, t).start()
            ag1_copy(b, g, 1 - b, 0).start()
            stage[g][b, b, pos] = pack[g][b]

    def ag2(b, g):
        for t in range(1, first):
            ag1_landing(b, g, t).wait_recv()

        @pl.when(core != b)
        def _():
            ag1_landing(b, g, 0).wait_recv()

        for t in range(1, rest):
            ag2_copy(b, g, t).start()

    def ag3(b, g):
        for t in range(1, rest):
            ag2_copy(b, g, t).wait_recv()
        for t in range(1, rest):
            ag3_copy(b, g, t).start()
        ag4_copy(b, g, 0).start()

    def ag4(b, g):
        for t in range(1, rest):
            ag3_copy(b, g, t).wait_recv()
            ag4_copy(b, g, t).start()

    def ag5(b, g):
        for t in range(rest):
            ag4_landing(b, g, t).wait_recv()
        lay_out(b, g)

    def ag_sent(b, g):
        @pl.when(core == b)
        def _():
            for t in range(1, first):
                for half in range(2):
                    ag1_copy(b, g, half, t).wait_send()
            ag1_copy(b, g, 1 - b, 0).wait_send()

        for t in range(1, rest):
            ag2_copy(b, g, t).wait_send()
            ag3_copy(b, g, t).wait_send()
        for t in range(rest):
            ag4_copy(b, g, t).wait_send()

    def lay_out(b, g):
        if g == TAB:
            table_in(b)
            return
        if g == DOWN:
            for j in range(n):
                for half in range(2):
                    begin = 4 * unit * j + 2 * unit * half
                    wdown[b, begin : begin + 2 * unit, :] = s_d[b, half, place(half, j)]
            return
        together = 16 // math.gcd(unit, 16)
        for half in range(2):
            for j in range(0, n, together):
                pieces = [stage[g][b, half, place(half, j + i)].astype(F32) for i in range(together)]
                for sub in range(2):
                    low = sub * unit
                    block = jnp.concatenate([piece[low : low + unit] for piece in pieces], axis=0).astype(LOW)
                    part = 2 * half + sub
                    down = slice(unit * j, unit * (j + together))
                    if g == UP:
                        wup[b, down, part * width : (part + 1) * width] = block
                    elif part == 3:
                        wout[b, down, :] = block
                    else:
                        wqkv[b, down, part * width : (part + 1) * width] = block

    def rs0_copy(b, g):
        return remote(stage[g].at[b, 1 - core], r0[g], rs0_s.at[at(b, g)], rs0_r.at[at(b, g)], sibling)

    def rs1_copy(b, g, t):
        return remote(
            stage[g].at[b, core, slab_three((dig_three + t) % rest)], r1[g].at[t - 1],
            rs1_s.at[at(b, g), t - 1, 0], rs1_r.at[at(b, g), t - 1, 0], peer_three(t),
        )

    def rs2_copy(b, g, t):
        return remote(
            stage[g].at[b, core, slab_two(dig_three, (dig_two + t) % rest)], r2[g].at[b, t - 1],
            rs2_s.at[at(b, g), t - 1], rs2_r.at[at(b, g), t - 1], peer_two(t),
        )

    def rs3_copy(b, g, t):
        there = (dig_three * rest + dig_two) * first + (dig_a + t) % first
        device = {"section": b, **peer_first(t)} if t else sibling
        return remote(
            stage[g].at[b, core, there], r3[g].at[core, t], rs3_s.at[at(b, g), t], rs3_r.at[g, core, t], device
        )

    chunk_count = 2 if first % 2 == 0 else 1
    chunk_size = first // chunk_count

    def plane_copy(b, g, t, part):
        three, two = plane[t]
        begin = (((dig_three + three) % rest) * rest + (dig_two + two) % rest) * first + chunk_size * part
        return remote(
            stage[g].at[b, core, pl.ds(begin, chunk_size)], r1[g].at[t, pl.ds(chunk_size * part, chunk_size)],
            rs1_s.at[at(b, g), t, part], rs1_r.at[at(b, g), t, part], peer_plane(three, two),
        )

    def rs0(b, g):
        @pl.when(b == 0)
        def _():
            pl.semaphore_wait(credit.at[0, g], 1)

        rs0_copy(b, g).start()

    def rs1(b, g):
        rs0_copy(b, g).wait_recv()

        @pl.loop(0, n)
        def _(p):
            stage[g][b, core, p] = stage[g][b, core, p] + r0[g][p]

        @pl.when(b == 1)
        def _():
            pl.semaphore_signal(credit.at[0, g], inc=1, device_id=sibling, device_id_type=pl.DeviceIdType.MESH)

        direct = g in (ATT, TAB)
        if rest > 1:
            @pl.when(b == 0)
            def _():
                pl.semaphore_wait(credit.at[1, g], len(plane) if direct else rest - 1)

        if direct:
            for part in range(chunk_count):
                for t in range(len(plane)):
                    plane_copy(b, g, t, part).start()
            return
        for t in range(1, rest):
            rs1_copy(b, g, t).start()

    def rs2(b, g):
        for t in range(1, rest):
            rs1_copy(b, g, t).wait_recv()

        @pl.loop(0, rest * first)
        def _(p):
            here = dig_three * rest * first + p
            total = stage[g][b, core, here].astype(F32)
            for t in range(1, rest):
                total = total + r1[g][t - 1, p].astype(F32)
            stage[g][b, core, here] = total.astype(stage[g].dtype)

        for t in range(1, rest):
            @pl.when(b == 1)
            def _():
                pl.semaphore_signal(
                    credit.at[1, g], inc=1, device_id=peer_three(t), device_id_type=pl.DeviceIdType.MESH
                )

            rs2_copy(b, g, t).start()

    def rs3_send(b, g, part):
        def here(digit):
            return (digit >= chunk_size * part) & (digit < chunk_size * (part + 1))

        for t in range(1, first):
            @pl.when(here((dig_a + t) % first))
            def _():
                rs3_copy(b, g, t).start()

        @pl.when(here(dig_a) & (core != b))
        def _():
            rs3_copy(b, g, 0).start()

    def rs3_part(b, g, part):
        for t in range(len(plane)):
            plane_copy(b, g, t, part).wait_recv()

        @pl.loop(chunk_size * part, chunk_size * (part + 1))
        def _(p):
            here = (dig_three * rest + dig_two) * first + p
            total = stage[g][b, core, here].astype(F32)
            for t in range(len(plane)):
                total = total + r1[g][t, p].astype(F32)
            stage[g][b, core, here] = total.astype(stage[g].dtype)

        rs3_send(b, g, part)

    def rs3_first(b, g):
        rs3_part(b, g, 0)

    def rs3_rest(b, g):
        for part in range(1, chunk_count):
            rs3_part(b, g, part)

    def rs3(b, g):
        if g in (ATT, TAB):
            for part in range(chunk_count):
                rs3_part(b, g, part)

            @pl.when(b == 1)
            def _():
                for three, two in plane:
                    pl.semaphore_signal(
                        credit.at[1, g], inc=1, device_id=peer_plane(three, two),
                        device_id_type=pl.DeviceIdType.MESH,
                    )

            return
        for t in range(1, rest):
            rs2_copy(b, g, t).wait_recv()

        @pl.loop(0, first)
        def _(p):
            here = (dig_three * rest + dig_two) * first + p
            total = stage[g][b, core, here].astype(F32)
            for t in range(1, rest):
                total = total + r2[g][b, t - 1, p].astype(F32)
            stage[g][b, core, here] = total.astype(stage[g].dtype)

        for part in range(chunk_count):
            rs3_send(b, g, part)

    def rs4(b, g):
        @pl.when(core == b)
        def _():
            for own in (True, False):
                half = core if own else 1 - core
                begin = int(own)
                for t in range(begin, first):
                    ref = r3[g].at[half, t]
                    remote(ref, ref, rs3_s.at[at(b, g), t], rs3_r.at[g, half, t], sibling).wait_recv()
                total = stage[g][b, core, pos].astype(F32) if own else None
                for t in range(begin, first):
                    value = r3[g][half, t].astype(F32)
                    total = value if total is None else total + value
                final[g][half] = total

    def rs_sent(b, g):
        rs0_copy(b, g).wait_send()
        if g in (ATT, TAB):
            for part in range(chunk_count):
                for t in range(len(plane)):
                    plane_copy(b, g, t, part).wait_send()
        else:
            for t in range(1, rest):
                rs1_copy(b, g, t).wait_send()
                rs2_copy(b, g, t).wait_send()
        for t in range(1, first):
            rs3_copy(b, g, t).wait_send()

        @pl.when(core != b)
        def _():
            rs3_copy(b, g, 0).wait_send()

    def rows_of(i, images_too=1):
        return pl.ds(pl.multiple_of(i * rows, 16), images_too * rows)

    few = TOGETHER if slots % TOGETHER == 0 else 1
    many = TOGETHER_ROWS if slots % TOGETHER_ROWS == 0 else 1

    def step_rows(i, count):
        return rows_of(i * count, count)

    def ship_parts(kind, b, i):
        src, out = (io_one, io_two)[kind].at[i], out_far.at[kind, core, i]
        q = 2 * kind + b
        near = pltpu.make_async_copy(src, out, ship_s.at[q, i])
        far = remote(src, out, ship_s.at[q, i], ship_r.at[q, i], sibling)
        return near, far

    def ship(kind, b, i):
        near, far = ship_parts(kind, b, i)

        @pl.when(core == b)
        def _():
            near.start()

        @pl.when(core != b)
        def _():
            far.start()

    def shipped(kind, b, i):
        near, far = ship_parts(kind, b, i)

        @pl.when(core == b)
        def _():
            near.wait()

        @pl.when(core != b)
        def _():
            far.wait_send()

    def landed(kind, b, i):
        q = 2 * kind + b
        ref = out_far.at[kind, 1 - core, i]

        @pl.when(core == b)
        def _():
            remote(ref, ref, ship_s.at[q, i], ship_r.at[q, i], sibling).wait_recv()

    def live(i):
        return jnp.where(i < counts[0, core], 1.0, 0.0).astype(F32)

    def only_live(i, value, count):
        parts = [value[rows * m : rows * (m + 1)] * live(i * count + m) for m in range(count)]
        return jnp.concatenate(parts, axis=0)

    def coming(which, i):
        slot = (which * slots + i) % raw.shape[0]
        return pltpu.make_async_copy((images, cotangent)[which].at[i], raw.at[slot], in_s.at[which, i])

    def take_in(which, i):
        coming(which, i).wait()
        both = raw[(which * slots + i) % raw.shape[0]].astype(F32)
        (io_one, io_two)[which][i] = jnp.where(core == 0, both[:, 0, :], both[:, 1, :]).astype(LOW)

    def weave(todo):
        ring = raw.shape[0]
        count = 2 * slots

        def fetch(t, m):
            source = out_far.at[t // slots, m, t % slots]
            return pltpu.make_async_copy(source, io_one.at[2 * (t % ring) + m], weave_in.at[m, t])

        def leave(t):
            return pltpu.make_async_copy(raw.at[t % ring], woven.at[t // slots, t % slots], weave_out.at[t])

        for t in range(ring - 1):
            for m in range(2):
                fetch(t, m).start()

        @pl.loop(0, count)
        def _(t):
            for when, act in todo.items():
                @pl.when(t == when)
                def _():
                    act()

            @pl.when(t + ring - 1 < count)
            def _():
                for m in range(2):
                    fetch(t + ring - 1, m).start()

            @pl.when(t >= ring)
            def _():
                leave(t - ring).wait()

            for m in range(2):
                fetch(t, m).wait()
                raw[t % ring, :, m, :] = io_one[2 * (t % ring) + m]
            leave(t).start()

        for t in range(count - ring, count):
            leave(t).wait()

    def far_copy(which, i, back):
        near, far = ((hid, hid_far), (slope, slope_far))[which]
        near, far = near.at[rows_of(i)], far.at[rows_of(i)]
        src, dst = (far, near) if back else (near, far)
        return pltpu.make_async_copy(src, dst, far_s.at[2 * int(back) + which, i])

    pairs = width // 128
    scale = head_dim ** -0.5
    lane = lax.broadcasted_iota(jnp.int32, (1, 128), 1)
    half_low = [(lane < head_dim).astype(LOW), (lane >= head_dim).astype(LOW)]
    half_f = [(lane < head_dim).astype(F32), (lane >= head_dim).astype(F32)]
    token = lax.broadcasted_iota(jnp.int32, (rows, 128), 0) < length
    half_valid = [jnp.where(token, half_f[j], 0.0).astype(LOW) for j in range(2)]
    valid_lanes = jnp.where(lax.broadcasted_iota(jnp.int32, (1, rows), 1) < length, 1.0, 0.0).astype(F32)
    spare = -rows % 128
    chunk = 2 * width
    chunks = ff // chunk

    def vec(s, r):
        return table[s, r : r + 1, :]

    def up_bias(s, c):
        begin = c * chunk
        row, col = begin // width, begin % width
        if col + chunk <= width:
            return table[s, BU + row : BU + row + 1, col : col + chunk]
        a = table[s, BU + row : BU + row + 1, col:width]
        b = table[s, BU + row + 1 : BU + row + 2, 0 : chunk - (width - col)]
        return jnp.concatenate([a, b], axis=1)

    def add_vec(s, r, value):
        gtable[s, r : r + 1, :] += value

    def attn_forward(s, x, hat, i):
        rd = step_rows(i, few)
        nrm_ref, qkv_ref, prob_ref, ctx_ref = nrm1.at[s], qkv.at[s], prob.at[s], ctx.at[s]
        nrm = (hat * vec(s, G1) + vec(s, S1)).astype(LOW)
        nrm_ref[rd, :] = nrm
        mixed = mm(nrm, wqkv[s])
        q = (mixed[:, 0:width] + vec(s, BQ)).astype(LOW)
        k = mixed[:, width : 2 * width].astype(LOW)
        v = (mixed[:, 2 * width :] + vec(s, BV)).astype(LOW)
        qkv_ref[rd, 0:width] = q
        qkv_ref[rd, width : 2 * width] = k
        qkv_ref[rd, 2 * width :] = v
        images_out = []
        for m in range(few):
            mine = slice(rows * m, rows * (m + 1))
            parts = []
            for p in range(pairs):
                cols = slice(128 * p, 128 * p + 128)
                weights, sides = [], []
                for j in range(2):
                    keys = k[mine, cols] * half_low[j]
                    keys = jnp.concatenate([keys, keys[rows - spare :]], axis=0)
                    scores = mm_right(q[mine, cols], keys)
                    top = jnp.max(scores, axis=-1, keepdims=True)
                    e = jnp.exp2((scores - top) * (scale * 1.4426950408889634)).astype(LOW)
                    prob_ref[i * few + m, 2 * p + j] = e[:, :rows]
                    weights.append(e)
                    sides.append(jnp.concatenate([v[mine, cols] * half_valid[j], half_valid[j]], axis=1))
                    sides.append(jnp.zeros((spare, 256), LOW))
                total = mm(jnp.concatenate(weights, axis=1), jnp.concatenate(sides, axis=0))
                over = 1.0 / total[:, 128:]
                overs[s, rows_of(i * few + m), cols] = over.astype(LOW)
                parts.append((total[:, :128] * over).astype(LOW))
            images_out.append(jnp.concatenate(parts, axis=1))
        context = jnp.concatenate(images_out, axis=0)
        ctx_ref[rd, :] = context
        return x + mm(context, wout[s]) + vec(s, BO)

    def ff_forward(s, after, rd):
        hat, rstd, _ = normalize(after)
        hat2[s, rd, :] = hat.astype(LOW)
        nrm = (hat * vec(s, G2) + vec(s, S2)).astype(LOW)
        total = after + vec(s, BD)
        for c in range(chunks):
            cols = slice(chunk * c, chunk * c + chunk)
            pre = mm(nrm, wup[s, :, cols]) + up_bias(s, c)
            phi, slo = normal_parts(pre)
            h = (pre * phi).astype(LOW)
            hid[rd, cols] = h
            slope[rd, cols] = slo.astype(LOW)
            total = total + mm(h, wdown[s, cols, :])
        return total, rstd

    def ff_backward(s, g, rd, rstd):
        g_low = g.astype(LOW)
        add_vec(s, BD, colsum(g_low.astype(F32)))
        d_nrm = None
        for c in range(chunks):
            cols = slice(chunk * c, chunk * c + chunk)
            d_hid = mm_right(g_low, wdown[s, cols, :])
            d_pre = (d_hid * slope[rd, cols].astype(F32)).astype(LOW)
            slope[rd, cols] = d_pre
            part = mm_right(d_pre, wup[s, :, cols])
            d_nrm = part if d_nrm is None else d_nrm + part
        hat = hat2[s, rd, :].astype(F32)
        add_vec(s, G2, colsum(d_nrm * hat))
        add_vec(s, S2, colsum(d_nrm))
        d_after = g + normalize_back(d_nrm * vec(s, G2), hat, rstd)
        low = d_after.astype(LOW)
        dal[rd, :] = low
        return d_after

    def attn_backward(s, i):
        qkv_ref, prob_ref, ctx_ref = qkv.at[s], prob.at[s], ctx.at[s]
        rd = step_rows(i, few)
        d_context = mm_right(dal[rd, :], wout[s])
        d_context = (d_context * overs[s, rd, :].astype(F32)).astype(LOW)
        for m in range(few):
            rd = rows_of(i * few + m)
            d_ctx = d_context[rows * m : rows * (m + 1)]
            dq, dk, dv = [], [], []
            for p in range(pairs):
                cols = slice(128 * p, 128 * p + 128)
                q = qkv_ref[rd, 128 * p : 128 * p + 128]
                k = qkv_ref[rd, width + 128 * p : width + 128 * p + 128]
                v = qkv_ref[rd, 2 * width + 128 * p : 2 * width + 128 * p + 128]
                dc = d_ctx[:, cols]
                both = dc.astype(F32) * ctx_ref[rd, cols].astype(F32)
                q_t, dc_t = q.T, dc.T
                to_q, to_k, to_v = None, [], []
                for j in range(2):
                    e = prob_ref[i * few + m, 2 * p + j]
                    delta = jnp.sum(both * half_f[j], axis=-1, keepdims=True)
                    d_prob = mm_right(dc, v * half_low[j])
                    ds = (e.astype(F32) * (d_prob - delta)).astype(LOW)
                    part = mm(ds, k * half_valid[j])
                    to_q = part if to_q is None else to_q + part
                    head = slice(head_dim * j, head_dim * (j + 1))
                    to_k.append(mm(q_t[head], ds))
                    to_v.append(mm(dc_t[head], e))
                dq.append((to_q * scale).astype(LOW))
                dk.append((jnp.concatenate(to_k, axis=0) * (valid_lanes * scale)).astype(LOW).T)
                dv.append((jnp.concatenate(to_v, axis=0) * valid_lanes).astype(LOW).T)
            d_mixed = jnp.concatenate(dq + dk + dv, axis=1)
            qkv_ref[rd, :] = d_mixed

    def input_backward(s, d_after, rd, x, mean, rstd):
        d_nrm = mm_right(qkv[s, rd, :], wqkv[s])
        hat = (x - mean) * rstd
        add_vec(s, G1, colsum(d_nrm * hat))
        add_vec(s, S1, colsum(d_nrm))
        return d_after + normalize_back(d_nrm * vec(s, G1), hat, rstd)

    def grads_down(s):
        left_t[0:width, :] = low_g[...].T

        @pl.loop(0, 2)
        def _(c):
            cols = pl.ds(pl.multiple_of(c * 2 * width, 128), 2 * width)
            block = mm(left_t[0:width, :], hid[:, cols]).T
            for i in range(n // 2):
                for half in range(2):
                    begin = 4 * unit * i + 2 * unit * half
                    s_d[s, half, place(half, c * (n // 2) + i)] = block[begin : begin + 2 * unit].astype(LOW)

    def pair_out(ref, s, half, one, two):
        for j in range(n):
            down = slice(unit * j, unit * (j + 1))
            piece = jnp.concatenate([one[down], two[down]], axis=0).astype(LOW)
            ref[s, half, place(half, j)] = piece

    def grads_up(s):
        left_t[0:width, :] = (hat2[s].astype(F32) * vec(s, G2) + vec(s, S2)).astype(LOW).T
        for half in range(2):
            both = mm(left_t[...], slope[:, 2 * half * width : 2 * (half + 1) * width])
            pair_out(s_u, s, half, both[:, :width], both[:, width:])
            gtable[s, BU + 2 * half : BU + 2 * half + 1, :] = both[width : width + 1, :width]
            gtable[s, BU + 2 * half + 1 : BU + 2 * half + 2, :] = both[width : width + 1, width:]

    def grads_attn(s):
        mix_s = qkv.at[s]
        left_t[0:width, :] = ctx[s].T
        four = mm(left_t[...], dal[...])
        left_t[0:width, :] = nrm1[s].T
        three = mm(left_t[...], mix_s[:, 2 * width :])
        pair_out(s_a, s, 1, three, four)
        both = mm(left_t[...], mix_s[:, 0 : 2 * width])
        pair_out(s_a, s, 0, both[:, :width], both[:, width:])
        for row, sums in ((BO, four), (BV, three), (BQ, both)):
            gtable[s, row : row + 1, :] = sums[width : width + 1, :width]

    barrier = pltpu.get_barrier_semaphore()
    greeted = [sibling]
    greeted += [{"section": half, **peer_first(t)} for t in range(1, first) for half in range(2)]
    greeted += [peer_plane(three, two) for three, two in plane]
    for device in greeted:
        pl.semaphore_signal(barrier, inc=1, device_id=device, device_id_type=pl.DeviceIdType.MESH)
    pack_own()
    pl.semaphore_wait(barrier, len(greeted))

    def run(*todo):
        for f, b, g in todo:
            f(b, g)

    def events(i, table_of):
        for when, todo in table_of.items():
            @pl.when(i == when)
            def _():
                run(*todo)

    def both(f, b, g):
        return [(f, b, g), (f, b, TAB)]

    def take(i, m):
        return pl.ds(pl.multiple_of((i * many + m) * rows, 16), length)

    ahead = raw.shape[0]
    run(*both(ag1, 0, ATT))
    for i in range(ahead):
        coming(0, i).start()
    fill_repeats()
    gtable[...] = jnp.zeros_like(gtable)
    left_t[width:, :] = jnp.ones((16, left_t.shape[1]), LOW)
    low_g[...] = jnp.zeros_like(low_g)
    xs[0] = jnp.zeros_like(low_g)

    @pl.loop(0, slots)
    def images_in(i):
        take_in(0, i)

        @pl.when(i + ahead < slots)
        def _():
            coming(0, i + ahead).start()

        @pl.when(i + ahead >= slots)
        def _():
            coming(1, i + ahead - slots).start()

        @pl.when(i == 4)
        def _():
            run((ag1, 0, UP))

    run(*both(ag2, 0, ATT), (ag1, 0, DOWN), *both(ag1, 1, ATT))

    def statistic(s, rd, which):
        return jnp.where(s == 0, rstds[rd, which : which + 1], rstds[rd, 3 + which : 4 + which])

    def first_norm(s, rd, x):
        hat, rstd, mean = normalize(x)
        after_ref[rd, :] = hat
        rstds[rd, 3 * s : 3 * s + 1] = rstd
        rstds[rd, 3 * s + 2 : 3 * s + 3] = mean

    @pl.loop(0, slots // many)
    def norm_one(i):
        for m in range(many):
            xs[0, take(i, m), :] = io_one[i * many + m]
        rd = step_rows(i, many)
        x = xs[0, rd, :].astype(F32)
        token_rows = lax.broadcasted_iota(jnp.int32, (rows, width), 0) < length
        parts = [x[rows * m : rows * (m + 1)] for m in range(many)]
        x = jnp.concatenate([jnp.where(token_rows, part, part[0:1]) for part in parts], axis=0)
        xs[0, rd, :] = x.astype(LOW)
        first_norm(0, rd, x)

    run((ag2, 0, UP), *both(ag3, 0, ATT), (ag1, 1, UP), (ag1, 1, DOWN), (ag2, 0, DOWN), (ag3, 0, UP))

    @pl.loop(0, slots)
    def cotangents_in(i):
        take_in(1, i)

        @pl.when(i + ahead < slots)
        def _():
            coming(1, i + ahead).start()

    run(*both(ag4, 0, ATT), (ag3, 0, DOWN), *both(ag2, 1, ATT), *both(ag5, 0, ATT))

    @pl.loop(0, 2)
    def forward(s):
        @pl.loop(0, slots // few)
        def attention(i):
            @pl.when(s == 0)
            def _():
                events(i, {1: [(ag4, 0, UP), (ag2, 1, UP)], 2: [(ag4, 0, DOWN)]})

            @pl.when(s == 1)
            def _():
                events(i, {1: [(ag4, 1, UP)], 2: [(ag4, 1, DOWN)]})

            rd = step_rows(i, few)
            after_ref[rd, :] = attn_forward(s, xs[s, rd, :].astype(F32), after_ref[rd, :], i)

        @pl.when(s == 0)
        def _():
            run(*both(ag3, 1, ATT), (ag5, 0, UP), (ag5, 0, DOWN))

        @pl.when(s == 1)
        def _():
            run((ag5, 1, UP), (ag5, 1, DOWN))

        @pl.loop(0, slots // many)
        def feed_forward(i):
            @pl.when(s == 0)
            def _():
                events(i, {0: [(ag2, 1, DOWN), (ag3, 1, UP)], 2: both(ag4, 1, ATT)})

            rd = step_rows(i, many)

            @pl.when(s == 1)
            def _():
                for m in range(many):
                    far_copy(0, i * many + m, False).wait()
                    far_copy(1, i * many + m, False).wait()
                    shipped(0, 0, i * many + m)

            out, rstd2 = ff_forward(s, after_ref[rd, :], rd)
            for block in range(2):
                @pl.when(s == block)
                def _():
                    rstds[rd, 3 * block + 1 : 3 * block + 2] = rstd2

            out = only_live(i, out, many)
            for m in range(many):
                io_one[i * many + m] = out[rows * m : rows * m + length].astype(LOW)
                ship(0, s, i * many + m)

            @pl.when(s == 0)
            def _():
                for m in range(many):
                    far_copy(0, i * many + m, False).start()
                    far_copy(1, i * many + m, False).start()
                low = out.astype(LOW)
                xs[1, rd, :] = low
                first_norm(1, rd, low.astype(F32))

        @pl.when(s == 0)
        def _():
            run((ag3, 1, DOWN), *both(ag5, 1, ATT))

    for b in range(2):
        for g in groups:
            ag_sent(b, g)

    @pl.loop(0, 2)
    def backward(turn):
        s = 1 - turn

        @pl.loop(0, slots // many)
        def feed_forward(i):
            @pl.when(s == 0)
            def _():
                events(i, {1: [*both(rs1, 1, ATT), (rs3, 1, DOWN)], 2: [(rs3, 1, UP)]})
                for m in range(many):
                    far_copy(1, i * many + m, True).wait()

            rd = step_rows(i, many)
            for m in range(many):
                g = live(i * many + m) * io_two[i * many + m].astype(F32)
                low_g[take(i, m), :] = g.astype(LOW)
            after_ref[rd, :] = ff_backward(s, low_g[rd, :].astype(F32), rd, statistic(s, rd, 1))

        @pl.when(s == 0)
        def _():
            for i in range(slots):
                far_copy(0, i, True).wait()

        grads_down(s)
        run((rs0, s, DOWN))

        @pl.when(s == 1)
        def _():
            for i in range(slots):
                far_copy(0, i, True).start()

        grads_up(s)
        run((rs0, s, UP))

        @pl.when(s == 1)
        def _():
            for i in range(slots):
                far_copy(1, i, True).start()

        @pl.loop(0, slots // few)
        def attention(i):
            @pl.when(s == 0)
            def _():
                events(i, {1: both(rs3, 1, ATT)})

            events(i, {0: [(rs1, s, DOWN)], 1: [(rs1, s, UP)]})
            attn_backward(s, i)

        run((rs2, s, DOWN))

        @pl.when(s == 0)
        def _():
            run(*both(rs4, 1, ATT), (rs4, 1, DOWN), (rs4, 1, UP))

        grads_attn(s)
        run((rs0, s, ATT))

        @pl.loop(0, slots // many)
        def to_input(i):
            rd = step_rows(i, many)
            x = xs[s, rd, :].astype(F32)
            d_in = input_backward(s, after_ref[rd, :], rd, x, statistic(s, rd, 2), statistic(s, rd, 0))
            for m in range(many):
                @pl.when(s == 0)
                def _():
                    shipped(1, 1, i * many + m)

                io_two[i * many + m] = d_in[rows * m : rows * m + length].astype(LOW)
                ship(1, s, i * many + m)

        table_out(s)
        run((rs0, s, TAB), (rs2, s, UP))

    def sent_and_landed(kind):
        @pl.loop(0, slots)
        def _(i):
            shipped(kind, 1 - kind, i)
            for b in range(2):
                landed(kind, b, i)

    sent_and_landed(0)
    weave({
        1: lambda: run(*both(rs1, 0, ATT), (rs3, 0, DOWN)),
        3: lambda: run((rs3, 0, UP)),
        slots - raw.shape[0] + 1: lambda: sent_and_landed(1),
        slots: lambda: run(*both(rs3_first, 0, ATT)),
        slots + 3: lambda: run(*both(rs3_rest, 0, ATT), (rs4, 0, DOWN), (rs4, 0, UP)),
    })
    run(*both(rs4, 0, ATT))
    for b in range(2):
        for g in groups:
            rs_sent(b, g)


def output_kernel(
    woven, far_a, far_u, far_d, far_t, o_acts, o_ings, o_g1, o_s1, o_qkv, o_qv, o_out, o_bo, o_g2, o_s2, o_up, o_bu, o_down, o_bd,
    passing, f_a, f_u, f_d, f_t, sems, grad_sems
):
    coming = [
        pltpu.make_async_copy(source, target, grad_sems.at[i])
        for i, (source, target) in enumerate(((far_a, f_a), (far_u, f_u), (far_d, f_d), (far_t, f_t)))
    ]
    for copy in coming:
        copy.start()
    arriving, leaving = [], []
    for which, target in enumerate((o_acts, o_ings)):
        for i in range(target.shape[0]):
            arriving.append(pltpu.make_async_copy(woven.at[which, i], passing.at[which, i], sems.at[0, which, i]))
            leaving.append(pltpu.make_async_copy(passing.at[which, i], target.at[i], sems.at[1, which, i]))
    for copy in arriving:
        copy.start()
    for one, two in zip(arriving, leaving):
        one.wait()
        two.start()
    for copy in coming:
        copy.wait()
    unit, width = o_out.shape[1:]
    for half in range(2):
        o_down[0, 2 * unit * half : 2 * unit * (half + 1), :] = f_d[half]
        for sub in range(2):
            part = 2 * half + sub
            cols = slice(part * width, (part + 1) * width)
            o_up[0, :, cols] = f_u[half, unit * sub : unit * (sub + 1), :]
            piece = f_a[half, unit * sub : unit * (sub + 1), :]
            if part == 3:
                o_out[0] = piece
            else:
                o_qkv[0, :, cols] = piece
    begin = 0
    for out in (o_g1, o_s1, o_bo, o_g2, o_s2, o_bd, o_qv):
        part = out.shape[1]
        out[...] = f_t[0, :, begin : begin + part]
        begin += part
    o_bu[...] = f_t[1, :, 0 : o_bu.shape[1]]
    for copy in leaving:
        copy.wait()


def local(
    images, cotangent, counts,
    ln1_gain, ln1_bias, w_qkv, b_qv, w_out, b_out, ln2_gain, ln2_bias, w_up, b_up, w_down, b_down,
):
    micro_count, slots, length, width = images.shape
    ff = w_up.shape[2]
    rows = -(-length // 16) * 16
    n = lax.axis_size("fsdp")
    unit = width // n
    first, rest = radices(n)
    total = slots * rows
    head_dim = width // HEADS

    def vm(*shape, kind=LOW):
        return pltpu.VMEM(shape, kind)

    tall = [(2 * unit, LOW)] * 3 + [(1, F32)]
    dma = lambda *shape: pltpu.SemaphoreType.DMA(shape)
    outs = [((2, slots, length, 2, width), LOW)]
    outs += [((2, r, width), F32) for r, _ in tall] + [((total, ff), LOW)] * 2 + [((2, 2, slots, length, width), LOW)]
    scratch = [
        vm(2, total, width), vm(3, length, 2, width), vm(slots, length, width), vm(slots, length, width),
        *[vm(2, r, width, kind=kind) for r, kind in tall],
        vm(2, width, 3 * width), vm(2, width, width), vm(2, width, ff), vm(2, ff, width),
        vm(2, TABLE, width, kind=F32), vm(2, TABLE, width, kind=F32),
        vm(unit, width), vm(2 * unit, 2 * width), vm(4 * unit, 4 * width),
        vm(total, width, kind=F32), vm(2, total, width), vm(2, total, 3 * width), vm(2, slots, HEADS, rows, rows),
        vm(2, total, width),
        vm(2, total, width), vm(2, total, width), vm(total, 6, kind=F32),
        vm(total, ff), vm(total, ff), vm(total, width), vm(total, width), vm(width + 16, total),
    ]
    scratch += [vm(2, 2, n, r, width, kind=kind) for r, kind in tall]
    scratch += [vm(n, r, width, kind=kind) for r, kind in tall]
    plane = rest * rest - 1
    for g, (r, kind) in enumerate(tall):
        direct = g in (ATT, TAB)
        scratch.append(vm(*((plane, first) if direct else (rest - 1, rest * first)), r, width, kind=kind))
    scratch += [vm(2, rest - 1, first, *tall[g][:1], width) for g in (UP, DOWN)]
    scratch += [vm(2, first, r, width, kind=kind) for r, kind in tall]
    scratch += [dma(2, slots), dma(2, 2 * slots), dma(2 * slots), dma(4, slots), dma(4, slots), dma(4, slots)]
    scratch += [dma(4, 2, first), dma(8, first)] + [dma(8, rest - 1)] * 4 + [dma(8, rest)] * 2
    scratch += [dma(8)] * 2 + [dma(8, plane, 2)] * 2 + [dma(8, rest - 1)] * 2 + [dma(8, first), dma(4, 2, first)]
    scratch += [pltpu.SemaphoreType.REGULAR((2, 4))]
    dims = (slots, length, rows, width, ff, head_dim, n)
    vmem = pl.BlockSpec(memory_space=pltpu.VMEM)
    hbm = pl.BlockSpec(memory_space=pltpu.HBM)
    woven, f_a, f_u, f_d, f_t, *_ = pl.pallas_call(
        functools.partial(whole_kernel, dims),
        out_shape=[jax.ShapeDtypeStruct(*o) for o in outs],
        in_specs=[hbm, hbm, pl.BlockSpec(memory_space=pltpu.SMEM)] + [vmem] * 12,
        out_specs=[hbm] + [vmem] * 4 + [hbm] * 3,
        scratch_shapes=scratch,
        compiler_params=pltpu.CompilerParams(
            vmem_limit_bytes=(64 << 20) - (96 << 10), collective_id=0, has_side_effects=True
        ),
    )(
        images.transpose(1, 2, 0, 3), cotangent.transpose(1, 2, 0, 3), counts.T, ln1_gain, ln1_bias, b_out, ln2_gain, ln2_bias, b_down, b_qv, b_up,
        w_qkv, w_out, w_up, w_down,
    )

    params = (
        ln1_gain, ln1_bias, w_qkv, b_qv, w_out, b_out, ln2_gain, ln2_bias, w_up, b_up, w_down, b_down
    )
    acts, ings, *grads = pl.pallas_call(
        output_kernel,
        out_shape=[jax.ShapeDtypeStruct(woven.shape[1:], LOW)] * 2
        + [jax.ShapeDtypeStruct(p.shape, F32) for p in params],
        in_specs=[hbm] * 5,
        out_specs=[hbm] * 2 + [vmem] * len(params),
        scratch_shapes=[
            vm(2, slots, length, 2, width), *[vm(2, r, width, kind=F32) for r, _ in tall], dma(2, 2, slots), dma(4)
        ],
        compiler_params=pltpu.CompilerParams(vmem_limit_bytes=(64 << 20) - (96 << 10)),
    )(woven, f_a, f_u, f_d, f_t)

    def as_given(value):
        return value.transpose(2, 0, 1, 3)[None]

    return (as_given(acts), as_given(ings), *grads)


def solution(mesh):
    split = P("section", "fsdp")
    cube = P("section", "fsdp", None)
    image = P(None, "fsdp", None, None)
    result = P("section", None, "fsdp", None, None)
    params = (split, split, cube, split, cube, split, split, split, cube, split, cube, split)
    return jax.shard_map(
        local,
        mesh=mesh,
        in_specs=(image, image, P(None, "fsdp")) + params,
        out_specs=(result, result) + params,
        check_vma=False,
    )
```

profile of v0, /device:TPU:0, one launch (start us, length us, event | category | flops | bytes accessed | tf_op | source)
XLA Modules:
  0.0 138.7 jit_solution(7144582134180948657)
XLA Ops:
  0.7 133.4 %shard_map.254 = (bf16[2,6,197,2,384]{4,3,2,1,0:T(2,128)(2,1)}, f32[2,48,384]{2,1,0:T(8,128)}, f32[2,48,384]{2,1,0:T(8,128)}, f32[2,48,384]{2,1,0:T(8,128)}, f32...) custom-call(bf16[6,197,2,384]{3,2,1,0:T(2,128)(2,1)} %bitcast.9, ...), custom_call_target="tpu_custom_call" | custom-call | tf_op jit(solution)/shard_map/pallas_call | solution.py:1094
  134.0 4.5 %shard_map.255 = (bf16[6,197,2,384]{3,2,1,0:T(2,128)(2,1)}, bf16[6,197,2,384]{3,2,1,0:T(2,128)(2,1)}, f32[1,24]{1,0:T(1,128)}, f32[1,24]{1,0:T(1,128)}, f32[1,24...) custom-call(bf16[2,6,197,2,384]{4,3,2,1,0:T(2,128)(2,1)} %get-tuple-, ...), custom_call_target="tpu_custom_call" | custom-call | tf_op jit(solution)/shard_map/pallas_call | solution.py:1111
where the time goes:
time: 139 us
  Pallas kernels  138 us (99%)
    pallas_call x1, Pallas kernels, local(): pl.pallas_call(functools.partial(whole_kernel, dims), out_shape=[jax.Shap...  133 us
    pallas_call x1, Pallas kernels, local(): pl.pallas_call(output_kernel, out_shape=[jax.ShapeDtypeStruct(woven.shape...  4.48 us

commit v1 on v0

--- a/solution.py
+++ b/solution.py
@@ -829,7 +829,7 @@
         xs[0, rd, :] = x.astype(LOW)
         first_norm(0, rd, x)
 
-    run((ag2, 0, UP), *both(ag3, 0, ATT), (ag1, 1, UP), (ag1, 1, DOWN), (ag2, 0, DOWN), (ag3, 0, UP))
+    run(*both(ag3, 0, ATT), (ag2, 0, UP), (ag1, 1, UP), (ag1, 1, DOWN))
 
     @pl.loop(0, slots)
     def cotangents_in(i):
@@ -839,7 +839,7 @@
         def _():
             coming(1, i + ahead).start()
 
-    run(*both(ag4, 0, ATT), (ag3, 0, DOWN), *both(ag2, 1, ATT), *both(ag5, 0, ATT))
+    run(*both(ag4, 0, ATT), (ag2, 0, DOWN), (ag3, 0, UP), *both(ag5, 0, ATT))
 
     @pl.loop(0, 2)
     def forward(s):
@@ -847,7 +847,9 @@
         def attention(i):
             @pl.when(s == 0)
             def _():
-                events(i, {1: [(ag4, 0, UP), (ag2, 1, UP)], 2: [(ag4, 0, DOWN)]})
+                events(i, {
+                    0: [(ag3, 0, DOWN), *both(ag2, 1, ATT)], 1: [(ag4, 0, UP), (ag2, 1, UP)], 2: [(ag4, 0, DOWN)],
+                })
 
             @pl.when(s == 1)
             def _():

time: 139 us -> 139 us (level)
  no operation moved by 1% of the time
where the time goes in v1:
time: 139 us
  Pallas kernels  138 us (99%)
    pallas_call x1, Pallas kernels, local(): pl.pallas_call(functools.partial(whole_kernel, dims), out_shape=[jax.Shap...  133 us
    pallas_call x1, Pallas kernels, local(): pl.pallas_call(output_kernel, out_shape=[jax.ShapeDtypeStruct(woven.shape...  4.48 us

profile of v1, /device:TPU:0, one launch (start us, length us, event | category | flops | bytes accessed | tf_op | source)
XLA Modules:
  0.0 138.6 jit_solution(18018174731449367680)
XLA Ops:
  0.7 133.3 %shard_map.254 = (bf16[2,6,197,2,384]{4,3,2,1,0:T(2,128)(2,1)}, f32[2,48,384]{2,1,0:T(8,128)}, f32[2,48,384]{2,1,0:T(8,128)}, f32[2,48,384]{2,1,0:T(8,128)}, f32...) custom-call(bf16[6,197,2,384]{3,2,1,0:T(2,128)(2,1)} %bitcast.9, ...), custom_call_target="tpu_custom_call" | custom-call | tf_op jit(solution)/shard_map/pallas_call | solution.py:1096
  134.0 4.5 %shard_map.255 = (bf16[6,197,2,384]{3,2,1,0:T(2,128)(2,1)}, bf16[6,197,2,384]{3,2,1,0:T(2,128)(2,1)}, f32[1,24]{1,0:T(1,128)}, f32[1,24]{1,0:T(1,128)}, f32[1,24...) custom-call(bf16[2,6,197,2,384]{4,3,2,1,0:T(2,128)(2,1)} %get-tuple-, ...), custom_call_target="tpu_custom_call" | custom-call | tf_op jit(solution)/shard_map/pallas_call | solution.py:1113
